TPU v7x, 32 devices: a whole 2x2x4 slice. The times are simulated.
32 devices in a mesh: dp: 8 (over z, y), tensor: 4 (over x, core).
Axes of the slice: x: 2, y: 2, z: 4, core: 2. Of those that a mesh axis runs over, the one named last changes fastest.
Arguments:
- images: float32 [32, 197, 768], P('dp'), may hold values from -6 to 6
- counts: int32 [8], P('dp'), may hold values from 3 to 4, as said below
- qkv_weight: bfloat16 [2, 768, 3, 12, 64], P(None, 'dp', None, 'tensor'), may hold values from -0.21875 to 0.21875
- qv_bias: bfloat16 [2, 2, 12, 64], P(None, None, 'tensor', 'dp'), may hold values from -4 to 4
- out_weight: bfloat16 [2, 12, 64, 768], P(None, 'tensor', None, 'dp'), may hold values from -0.625 to 0.625
- up_weight: bfloat16 [2, 768, 3072], P(None, 'dp', 'tensor'), may hold values from -0.21875 to 0.21875
- up_bias: bfloat16 [2, 24, 128], P(None, 'tensor', 'dp'), may hold values from -4 to 4
- down_weight: bfloat16 [2, 3072, 768], P(None, 'tensor', 'dp'), may hold values from -0.109375 to 0.109375
- gains: bfloat16 [2, 2, 768], P(None, None, 'dp'), may hold values from 0.099609375 to 1.8984375
- shifts: bfloat16 [2, 4, 768], P(None, None, 'dp'), may hold values from -4 to 4
- cotangent: float32 [32, 197, 768], P('dp'), may hold values from -6 to 6
Outputs:
- activations: float32 [32, 197, 768], P('dp')
- input_grad: float32 [32, 197, 768], P('dp')
- qkv_grad: float32 [2, 768, 3, 12, 64], P(None, 'dp', None, 'tensor')
- qv_bias_grad: float32 [2, 2, 12, 64], P(None, None, 'tensor', 'dp')
- out_grad: float32 [2, 12, 64, 768], P(None, 'tensor', None, 'dp')
- up_grad: float32 [2, 768, 3072], P(None, 'dp', 'tensor')
- up_bias_grad: float32 [2, 24, 128], P(None, 'tensor', 'dp')
- down_grad: float32 [2, 3072, 768], P(None, 'tensor', 'dp')
- gains_grad: float32 [2, 2, 768], P(None, None, 'dp')
- shifts_grad: float32 [2, 4, 768], P(None, None, 'dp')
Inputs may be any that keep to these rules, and one draw needn't show every extreme that they name: counts[i] is 3 or 4; in every draw some index holds 4 live images and some index holds 3.
All inputs are finite; a program needn't handle non-finite values.
Results may differ from a plain program's by a relative error of at most 0.0003.
Values may be sent and summed in bfloat16 or wider, within the bound.
A program may use at most 192 MiB of HBM per device.

v0:
```python
import math
import jax
import jax.numpy as jnp
from jax import lax
from jax.sharding import PartitionSpec as P

epsilon = 1e-06
high = lax.Precision.HIGH
f32 = jnp.float32
bf16 = jnp.bfloat16


def weight_product(a, w, w_dim=0):
    top = lax.reduce_precision(a, 8, 7)
    rest = (a - top).astype(bf16)
    dims = (((1,), (w_dim,)), ((), ()))
    return lax.dot_general(top.astype(bf16), w, dims, preferred_element_type=f32) + lax.dot_general(
        rest, w, dims, preferred_element_type=f32
    )


def cross(a, b):
    return lax.dot_general(
        a, b, (((0,), (0,)), ((), ())), precision=high, preferred_element_type=f32
    )


def heads_product(spec, a, b):
    return jnp.einsum(spec, a, b, precision=high, preferred_element_type=f32)


def norm_keep(values, gain, shift):
    average = jnp.mean(values, axis=-1, keepdims=True)
    centered = values - average
    variance = jnp.mean(centered * centered, axis=-1, keepdims=True)
    inverse = lax.rsqrt(variance + epsilon)
    normed = centered * inverse
    return (normed * gain + shift, normed, inverse)


def norm_back(grad_out, normed, inverse, gain):
    scaled = grad_out * gain
    first_mean = jnp.mean(scaled, axis=-1, keepdims=True)
    second_mean = jnp.mean(scaled * normed, axis=-1, keepdims=True)
    return inverse * (scaled - first_mean - normed * second_mean)


def gelu_parts(hidden):
    normal_cdf = 0.5 * (1.0 + lax.erf(hidden / math.sqrt(2.0)))
    density = jnp.exp(-0.5 * hidden * hidden) / math.sqrt(2.0 * math.pi)
    return (hidden * normal_cdf, normal_cdf + hidden * density)


core_pairs = [(0, 1), (1, 0), (2, 3), (3, 2)]
chip_pairs = [(0, 2), (2, 0), (1, 3), (3, 1)]


def tensor_sum(partial):
    rows, width = partial.shape
    halves = partial.reshape(2, rows // 2, width)
    core = lax.rem(lax.axis_index("tensor"), 2)
    first = core == 0
    mine = jnp.where(first, halves[0], halves[1])
    other = jnp.where(first, halves[1], halves[0])
    mine = mine + lax.ppermute(other, "tensor", core_pairs)
    mine = mine + lax.ppermute(mine, "tensor", chip_pairs)
    other = lax.ppermute(mine, "tensor", core_pairs)
    return jnp.concatenate([jnp.where(first, mine, other), jnp.where(first, other, mine)])


def pack_small(rows_six, bias, up_bias):
    depth = rows_six.shape[1]
    flat = jnp.concatenate([bias.reshape(-1), up_bias.reshape(-1)])
    columns = -(-flat.shape[0] // depth)
    flat = jnp.pad(flat, (0, columns * depth - flat.shape[0])).reshape(columns, depth)
    block = jnp.concatenate([rows_six, flat]).T
    return jnp.pad(block, ((0, 0), (0, 128 - block.shape[1])))


def gather_weights(params, layer):
    qkv, bias, out, up, upb, down, gains, shifts = [p[layer] for p in params]
    depth, heads, head_dim = (qkv.shape[0], qkv.shape[2], qkv.shape[3])
    inner = heads * head_dim
    small = pack_small(jnp.concatenate([gains, shifts]), bias, upb)
    attention = jnp.concatenate(
        [qkv.reshape(depth, 3 * inner), out.reshape(inner, depth).T, small], axis=1
    )
    feed = jnp.concatenate([up, down.T], axis=1)
    attention = lax.all_gather(attention, "dp", axis=0, tiled=True)
    feed = lax.all_gather(feed, "dp", axis=0, tiled=True)
    width = attention.shape[0]
    n = width // depth
    small = attention[:, 4 * inner :].astype(f32).T
    bias_count, upb_count = (bias.size, upb.size)
    columns = -(-(bias_count + upb_count) // depth)
    flat = small[6 : 6 + columns].reshape(columns, n, depth).transpose(1, 0, 2).reshape(n, -1)
    bias_full = (
        flat[:, :bias_count].reshape((n,) + bias.shape).transpose(1, 2, 0, 3).reshape(2, 1, inner)
    )
    upb_full = (
        flat[:, bias_count : bias_count + upb_count]
        .reshape((n,) + upb.shape)
        .transpose(1, 0, 2)
        .reshape(1, -1)
    )
    ff = up.shape[1]
    return dict(
        qkv=attention[:, : 3 * inner],
        out=attention[:, 3 * inner : 4 * inner],
        up=feed[:, :ff],
        down=feed[:, ff:],
        gains=small[:2],
        shifts=small[2:6],
        bias=bias_full,
        upb=upb_full,
        heads=heads,
        head_dim=head_dim,
    )


def layer_forward(stream, w, tokens, padded):
    heads, head_dim = (w["heads"], w["head_dim"])
    inner = heads * head_dim
    rows = stream.shape[0]
    split = (rows // padded, padded, heads, head_dim)
    factor = 1.0 / math.sqrt(head_dim)
    h, normed, inverse = norm_keep(stream, w["gains"][0], w["shifts"][0])
    projected = weight_product(h, w["qkv"])
    q = (projected[:, :inner] + w["bias"][0]).reshape(split)
    k = projected[:, inner : 2 * inner].reshape(split)
    v = (projected[:, 2 * inner :] + w["bias"][1]).reshape(split)
    scores = heads_product("bqhe,bkhe->bhqk", q, k) * factor
    live = lax.broadcasted_iota(jnp.int32, (1, 1, 1, padded), 3) < tokens
    scores = jnp.where(live, scores, -jnp.inf)
    exponent = jnp.exp(scores - jnp.max(scores, axis=-1, keepdims=True))
    soft = exponent / jnp.sum(exponent, axis=-1, keepdims=True)
    mixed = heads_product("bhqk,bkhe->bqhe", soft, v).reshape(rows, inner)
    middle = stream + tensor_sum(weight_product(mixed, w["out"], 1)) + w["shifts"][2]
    h2, normed_two, inverse_two = norm_keep(middle, w["gains"][1], w["shifts"][1])
    hidden = weight_product(h2, w["up"]) + w["upb"]
    activated, slope = gelu_parts(hidden)
    result = middle + tensor_sum(weight_product(activated, w["down"], 1)) + w["shifts"][3]
    return (
        result,
        (normed, inverse, h, q, k, v, soft, mixed, normed_two, inverse_two, h2, activated, slope),
    )


def backward_feed(grad, w, stored):
    normed_two, inverse_two, h2, activated, slope = stored[8:]
    grad_hidden = weight_product(grad, w["down"]) * slope
    grad_norm = tensor_sum(weight_product(grad_hidden, w["up"], 1))
    middle = grad + norm_back(grad_norm, normed_two, inverse_two, w["gains"][1])
    feed = jnp.concatenate([cross(h2, grad_hidden), cross(grad, activated)], axis=1)
    sums = (
        jnp.sum(grad_norm * normed_two, axis=0),
        jnp.sum(grad_norm, axis=0),
        jnp.sum(grad, axis=0),
        jnp.sum(grad_hidden, axis=0),
    )
    return (middle, feed, sums)


def backward_attention(grad, w, stored, padded):
    normed, inverse, h, q, k, v, soft, mixed = stored[:8]
    heads, head_dim = (w["heads"], w["head_dim"])
    inner = heads * head_dim
    rows = grad.shape[0]
    split = (rows // padded, padded, heads, head_dim)
    factor = 1.0 / math.sqrt(head_dim)
    grad_mixed = weight_product(grad, w["out"])
    out_delta = cross(grad, mixed)
    shift_two = jnp.sum(grad, axis=0)
    dots = jnp.sum((grad_mixed * mixed).reshape(split), axis=-1).transpose(0, 2, 1)[..., None]
    grad_mixed = grad_mixed.reshape(split)
    grad_soft = heads_product("bqhe,bkhe->bhqk", grad_mixed, v)
    grad_v = heads_product("bhqk,bqhe->bkhe", soft, grad_mixed).reshape(rows, inner)
    grad_scores = soft * (grad_soft - dots) * factor
    grad_q = heads_product("bhqk,bkhe->bqhe", grad_scores, k).reshape(rows, inner)
    grad_k = heads_product("bhqk,bqhe->bkhe", grad_scores, q).reshape(rows, inner)
    projected = jnp.concatenate([grad_q, grad_k, grad_v], axis=1)
    grad_norm = tensor_sum(weight_product(projected, w["qkv"], 1))
    qkv_delta = cross(h, projected)
    sums = (
        jnp.sum(grad_norm * normed, axis=0),
        jnp.sum(grad_norm, axis=0),
        shift_two,
        jnp.stack([jnp.sum(grad_q, axis=0), jnp.sum(grad_v, axis=0)]),
    )
    grad_in = grad + norm_back(grad_norm, normed, inverse, w["gains"][0])
    return (grad_in, jnp.concatenate([qkv_delta, out_delta], axis=1), sums)


def shards(
    images,
    counts,
    qkv_weight,
    qv_bias,
    out_weight,
    up_weight,
    up_bias,
    down_weight,
    gains,
    shifts,
    cotangent,
):
    params = (qkv_weight, qv_bias, out_weight, up_weight, up_bias, down_weight, gains, shifts)
    slots, tokens, width = images.shape
    layers, depth = qkv_weight.shape[:2]
    n = width // depth
    padded = -(-tokens // 8) * 8
    present = (jnp.arange(slots) < counts[0]).astype(f32)[:, None, None]
    groups = 2
    per = slots // groups
    extend = ((0, 0), (0, padded - tokens), (0, 0))
    x_all = jnp.pad(images, extend)
    g_all = jnp.pad(cotangent * present, extend)
    weights = [gather_weights(params, layer) for layer in range(layers)]
    streams = [x_all[g * per : (g + 1) * per].reshape(per * padded, width) for g in range(groups)]
    grads = [g_all[g * per : (g + 1) * per].reshape(per * padded, width) for g in range(groups)]
    kept = []
    for layer in range(layers):
        both = [layer_forward(s, weights[layer], tokens, padded) for s in streams]
        streams = [b[0] for b in both]
        kept.append([b[1] for b in both])
    totals = [None] * layers
    for layer in reversed(range(layers)):
        w = weights[layer]
        both = [backward_feed(g, w, s) for g, s in zip(grads, kept[layer])]
        feed_total = lax.psum_scatter(
            sum((b[1] for b in both[1:])) + both[0][1], "dp", scatter_dimension=0, tiled=True
        )
        gain_one, shift_one, shift_three, upb_grad = [
            both[0][2][i] + both[1][2][i] for i in range(4)
        ]
        both = [backward_attention(b[0], w, s, padded) for b, s in zip(both, kept[layer])]
        grads = [b[0] for b in both]
        gain_zero, shift_zero, shift_two, bias_grad = [
            both[0][2][i] + both[1][2][i] for i in range(4)
        ]
        six = jnp.stack([gain_zero, gain_one, shift_zero, shift_one, shift_two, shift_three])
        bias_shape = (2, w["heads"], n, w["head_dim"] // n)
        upb_shape = (up_bias.shape[1], n, up_bias.shape[2])
        flat = jnp.concatenate(
            [
                bias_grad.reshape(bias_shape).transpose(2, 0, 1, 3).reshape(n, -1),
                upb_grad.reshape(upb_shape).transpose(1, 0, 2).reshape(n, -1),
            ],
            axis=1,
        )
        columns = -(-flat.shape[1] // depth)
        flat = jnp.pad(flat, ((0, 0), (0, columns * depth - flat.shape[1])))
        flat = flat.reshape(n, columns, depth).transpose(1, 0, 2).reshape(columns, width)
        small = jnp.concatenate([six, flat]).T
        small = jnp.pad(small, ((0, 0), (0, 128 - small.shape[1])))
        attention_total = lax.psum_scatter(
            jnp.concatenate([both[0][1] + both[1][1], small], axis=1),
            "dp",
            scatter_dimension=0,
            tiled=True,
        )
        totals[layer] = (attention_total, feed_total)
    heads, head_dim = qkv_weight.shape[3:]
    inner = heads * head_dim
    ff = up_weight.shape[2]
    collected = []
    for attention, feed in totals:
        small = attention[:, 4 * inner : 4 * inner + 128].T
        bias_count, upb_count = (qv_bias[0].size, up_bias[0].size)
        columns = -(-(bias_count + upb_count) // depth)
        flat = small[6 : 6 + columns].reshape(-1)
        collected.append(
            (
                attention[:, : 3 * inner].reshape(qkv_weight.shape[1:]),
                flat[:bias_count].reshape(qv_bias.shape[1:]),
                attention[:, 3 * inner : 4 * inner].T.reshape(out_weight.shape[1:]),
                feed[:, :ff],
                flat[bias_count : bias_count + upb_count].reshape(up_bias.shape[1:]),
                feed[:, ff:].T,
                small[:2],
                small[2:6],
            )
        )
    joined = [
        jnp.concatenate([s.reshape(per, padded, width) for s in part])[:, :tokens]
        for part in (streams, grads)
    ]
    return (joined[0] * present, joined[1]) + tuple(
        (jnp.stack([c[i] for c in collected]) for i in range(8))
    )


def solution(mesh):
    placed = (
        P("dp", None, None),
        P("dp"),
        P(None, "dp", None, "tensor", None),
        P(None, None, "tensor", "dp"),
        P(None, "tensor", None, "dp"),
        P(None, "dp", "tensor"),
        P(None, "tensor", "dp"),
        P(None, "tensor", "dp"),
        P(None, None, "dp"),
        P(None, None, "dp"),
        P("dp", None, None),
    )
    return jax.shard_map(
        shards,
        mesh=mesh,
        in_specs=placed,
        out_specs=(placed[0], placed[0]) + placed[2:10],
        check_vma=False,
    )
```

profile of v0, /device:TPU:0, one launch (start us, length us, event | category | flops | bytes accessed | tf_op | source)
XLA Modules:
  0.0 885.6 jit_solution(16186916780232538564)
XLA Ops:
  21.4 37.4 %all-gather.5.cloned.1.call-done = bf16[768,896]{1,0:T(8,128)(2,1)} async-done(((bf16[96,896]{1,0:T(8,128)(2,1)}), bf16[768,896]{1,0:T(8,128)(2,1)}) %all-gather.5.cloned.1.call-update) | async-done | bytes 1376272 | tf_op jit(solution)/shard_map/all_gather | solution.py:89
  61.7 2.2 fusion.67
  93.7 14.4 %collective-permute-done.1 = f32[200,768]{1,0:T(8,128)S(1)} collective-permute-done((f32[200,768]{1,0:T(8,128)S(1)}, f32[200,768]{1,0:T(8,128)S(1)}, u32[]{:S(2)}, u32[]{:S(2)}) %collective-permute-start.1) | collective-permute-done | bytes 614432 | tf_op jit(solution)/shard_map/ppermute | solution.py:66
  108.3 12.6 %collective-permute-done.13 = f32[200,768]{1,0:T(8,128)S(1)} collective-permute-done((f32[200,768]{1,0:T(8,128)S(1)}, f32[200,768]{1,0:T(8,128)S(1)}, u32[]{:S(2)}, u32[]{:S(2)}) %collective-permute-start.13) | collective-permute-done | bytes 614432 | tf_op jit(solution)/shard_map/ppermute | solution.py:66
  131.7 2.5 fusion.112
  154.1 12.8 %collective-permute-done.4 = f32[200,768]{1,0:T(8,128)} collective-permute-done((f32[200,768]{1,0:T(8,128)S(1)}, f32[200,768]{1,0:T(8,128)}, u32[]{:S(2)}, u32[]{:S(2)}) %collective-permute-start.4) | collective-permute-done | bytes 614432 | tf_op jit(solution)/shard_map/ppermute | solution.py:66
  172.1 7.0 collective-permute-done.16
  195.3 2.5 fusion.120
  242.0 6.5 collective-permute-done.7
  250.7 3.5 fusion.123
  254.2 6.7 collective-permute-done.19
  268.6 2.3 fusion.365
  282.4 3.0 subtract_multiply_fusion.3
  307.6 9.8 %collective-permute-done.10 = f32[200,768]{1,0:T(8,128)S(1)} collective-permute-done((f32[200,768]{1,0:T(8,128)S(1)}, f32[200,768]{1,0:T(8,128)S(1)}, u32[]{:S(2)}, u32[]{:S(2)}) %collective-permute-start.10) | collective-permute-done | bytes 614432 | tf_op jit(solution)/shard_map/ppermute | solution.py:66
  323.0 7.6 collective-permute-done.25
  332.1 5.1 fusion.82
  337.2 6.7 collective-permute-done.37
  345.2 11.3 %collective-permute-done.22 = f32[200,768]{1,0:T(8,128)} collective-permute-done((f32[200,768]{1,0:T(8,128)}, f32[200,768]{1,0:T(8,128)}, u32[]{:S(2)}, u32[]{:S(2)}) %collective-permute-start.22) | collective-permute-done | bytes 614432 | tf_op jit(solution)/shard_map/ppermute | solution.py:66
  364.0 2.5 multiply_reduce_fusion.1
  372.9 4.9 multiply_add_fusion.12
  386.5 2.5 fusion.16
  400.1 2.3 fusion.14
  425.7 2.2 reshape.2646
  452.7 2.5 broadcast_select_fusion.17
  475.4 2.4 pad_maximum_fusion.9
  479.5 3.0 fusion.84
  482.5 4.4 collective-permute-done.40
  488.4 3.1 fusion.86
  496.2 5.2 fusion.332
  502.9 4.9 fusion.345
  512.8 3.2 maximum_add_fusion.3
  516.1 3.4 select_maximum_fusion
  519.5 3.3 copy.682
  523.5 3.9 multiply_add_fusion.10
  538.4 2.6 fusion.81
  543.4 2.5 fusion.323
  546.0 11.9 %collective-permute-done.31 = f32[200,768]{1,0:T(8,128)S(1)} collective-permute-done((f32[200,768]{1,0:T(8,128)S(1)}, f32[200,768]{1,0:T(8,128)S(1)}, u32[]{:S(2)}, u32[]{:S(2)}) %collective-permute-start.31) | collective-permute-done | bytes 614432 | tf_op jit(solution)/shard_map/ppermute | solution.py:66
  558.1 2.7 fusion.327
  560.9 9.3 %collective-permute-done.43 = f32[200,768]{1,0:T(8,128)S(1)} collective-permute-done((f32[200,768]{1,0:T(8,128)S(1)}, f32[200,768]{1,0:T(8,128)S(1)}, u32[]{:S(2)}, u32[]{:S(2)}) %collective-permute-start.43) | collective-permute-done | bytes 614432 | tf_op jit(solution)/shard_map/ppermute | solution.py:66
  570.4 2.8 maximum_add_fusion.1
  573.2 6.1 copy.686
  584.2 4.5 multiply_add_fusion.8
  595.3 2.5 fusion.15
  607.7 2.3 fusion.394
  625.6 2.5 fusion.13
  632.8 2.5 convolution_bitcast_fusion.1
  638.5 2.3 fusion.396
  650.7 4.0 fusion.348
  654.8 4.5 fusion.398
  667.7 10.8 %collective-permute-done.34 = f32[200,768]{1,0:T(8,128)} collective-permute-done((f32[200,768]{1,0:T(8,128)}, f32[200,768]{1,0:T(8,128)}, u32[]{:S(2)}, u32[]{:S(2)}) %collective-permute-start.34) | collective-permute-done | bytes 614432 | tf_op jit(solution)/shard_map/ppermute | solution.py:66
  680.5 10.5 %collective-permute-done.46 = f32[200,768]{1,0:T(8,128)} collective-permute-done((f32[200,768]{1,0:T(8,128)}, f32[200,768]{1,0:T(8,128)}, u32[]{:S(2)}, u32[]{:S(2)}) %collective-permute-start.46) | collective-permute-done | bytes 614432 | tf_op jit(solution)/shard_map/ppermute | solution.py:66
  700.0 3.5 select_maximum_fusion.1
  703.4 3.3 copy.680
  707.0 4.3 fusion.404
  711.4 2.6 fusion.405
  714.0 2.7 fusion.85
  716.8 2.7 fusion.83
  719.5 2.7 maximum_add_fusion
  722.2 6.4 copy.684
  731.1 2.4 copy.642
  733.6 2.9 multiply_add_fusion.7
  736.7 2.4 copy.643
  744.0 32.7 %reduce-scatter.13.cloned.1.call-done = f32[96,896]{1,0:T(8,128)} async-done(((f32[768,896]{1,0:T(8,128)}), f32[96,896]{1,0:T(8,128)}) %reduce-scatter.13.cloned.1.call-update) | async-done | bytes 344080
  784.1 90.7 %reduce-scatter.17.cloned.1.call-done = f32[96,1536]{1,0:T(8,128)} async-done(((f32[768,1536]{1,0:T(8,128)}), f32[96,1536]{1,0:T(8,128)}) %reduce-scatter.17.cloned.1.call-update) | async-done | bytes 589840
  (1111 shorter events, 415.6 us)
Async XLA Ops:
  7.2 51.5 %all-gather.5.cloned.1.call-start = ((), (), s32[]{:S(2)}) async-start(), calls=%async_computation.4 | async-start | bytes 1548288 | tf_op jit(solution)/shard_map/all_gather | solution.py:89
  13.6 118.1 %all-gather.7.cloned.1.call-start = ((), (), s32[]{:S(2)}) async-start(), calls=%async_computation.5 | async-start | bytes 2654208 | tf_op jit(solution)/shard_map/all_gather | solution.py:90
  15.7 152.6 %all-gather.9.cloned.1.call-start = ((), (), s32[]{:S(2)}) async-start(), calls=%async_computation.6 | async-start | bytes 1548288 | tf_op jit(solution)/shard_map/all_gather | solution.py:89
  18.0 110.1 %copy-start = (f32[4,197,768]{2,1,0:T(8,128)}, f32[4,197,768]{2,1,0:T(8,128)S(1)}, u32[]{:S(2)}) copy-start(f32[4,197,768]{2,1,0:T(8,128)S(1)} %copy.540) | copy-start | bytes 7262212
  21.2 61.9 %copy-start.257 = (pred[200]{0:T(512)(128)(4,1)}, pred[200]{0:T(512)(128)(4,1)S(1)}, u32[]{:S(2)}) copy-start(pred[200]{0:T(512)(128)(4,1)S(1)} %iota_compare_fusion.4) | copy-start | bytes 604
  21.3 37.4 %copy-start.195 = (f32[2,200]{1,0:T(2,128)}, f32[2,200]{1,0:T(2,128)S(1)}, u32[]{:S(2)}) copy-start(f32[2,200]{1,0:T(2,128)S(1)} %add_rsqrt_fusion.3) | copy-start | bytes 4804
  60.9 82.8 %copy-start.166 = (f32[768]{0:T(1024)}, f32[768]{0:T(1024)S(1)}, u32[]{:S(2)}) copy-start(f32[768]{0:T(1024)S(1)} %get-tuple-element.100) | copy-start | bytes 9220
  60.9 82.8 %copy-start.193 = (f32[768]{0:T(1024)}, f32[768]{0:T(1024)S(1)}, u32[]{:S(2)}) copy-start(f32[768]{0:T(1024)S(1)} %get-tuple-element.99) | copy-start | bytes 9220
  79.1 10.5 %collective-permute-start = (f32[200,768]{1,0:T(8,128)}, f32[200,768]{1,0:T(8,128)}, u32[]{:S(2)}, u32[]{:S(2)}) collective-permute-start(f32[200,768]{1,0:T(8,128)} %slice_select_fusion.15), channel_id=1, source_target_pairs={{0,1},{1,0},{2,3},{3,2},{4,5},{5,4},{6,7},{7,6},{8,9},{9,8},{10,11... | collective-permute-start | bytes 1843208 | tf_op jit(solution)/shard_map/ppermute | solution.py:65
  89.0 3.9 collective-permute-start.12
  91.4 16.7 %collective-permute-start.1 = (f32[200,768]{1,0:T(8,128)S(1)}, f32[200,768]{1,0:T(8,128)S(1)}, u32[]{:S(2)}, u32[]{:S(2)}) collective-permute-start(f32[200,768]{1,0:T(8,128)S(1)} %select_add_fusion.15), channel_id=1, source_target_pairs={{0,2},{2,0},{1,3},{3,1},{4,6},{6,4},{5,7},{7,5},{8,10},{10,8},{9,1... | collective-permute-start | bytes 1843208 | tf_op jit(solution)/shard_map/ppermute | solution.py:66
  93.1 27.8 %collective-permute-start.13 = (f32[200,768]{1,0:T(8,128)S(1)}, f32[200,768]{1,0:T(8,128)S(1)}, u32[]{:S(2)}, u32[]{:S(2)}) collective-permute-start(f32[200,768]{1,0:T(8,128)S(1)} %select_add_fusion.11), channel_id=1, source_target_pairs={{0,2},{2,0},{1,3},{3,1},{4,6},{6,4},{5,7},{7,5},{8,10},{10,8},{9,1... | collective-permute-start | bytes 1843208 | tf_op jit(solution)/shard_map/ppermute | solution.py:66
  108.2 14.8 %collective-permute-start.2 = (f32[200,768]{1,0:T(8,128)S(1)}, f32[200,768]{1,0:T(8,128)}, u32[]{:S(2)}, u32[]{:S(2)}) collective-permute-start(f32[200,768]{1,0:T(8,128)S(1)} %add.1061), channel_id=1, source_target_pairs={{0,1},{1,0},{2,3},{3,2},{4,5},{5,4},{6,7},{7,6},{8,9},{9,8},{10,11... | collective-permute-start | bytes 1843208 | tf_op jit(solution)/shard_map/ppermute | solution.py:67
  121.8 2.4 collective-permute-start.14
  122.7 128.0 %all-gather.11.cloned.1.call-start = ((), (), s32[]{:S(2)}) async-start(), calls=%async_computation.7 | async-start | bytes 2654208 | tf_op jit(solution)/shard_map/all_gather | solution.py:90
  139.2 8.5 collective-permute-start.3
  147.6 3.9 collective-permute-start.15
  150.0 16.9 %collective-permute-start.4 = (f32[200,768]{1,0:T(8,128)S(1)}, f32[200,768]{1,0:T(8,128)}, u32[]{:S(2)}, u32[]{:S(2)}) collective-permute-start(f32[200,768]{1,0:T(8,128)S(1)} %select_add_fusion.14), channel_id=1, source_target_pairs={{0,2},{2,0},{1,3},{3,1},{4,6},{6,4},{5,7},{7,5},{8,10},{10,8},{9,1... | collective-permute-start | bytes 1843208 | tf_op jit(solution)/shard_map/ppermute | solution.py:66
  152.4 26.7 %collective-permute-start.16 = (f32[200,768]{1,0:T(8,128)}, f32[200,768]{1,0:T(8,128)}, u32[]{:S(2)}, u32[]{:S(2)}) collective-permute-start(f32[200,768]{1,0:T(8,128)} %select_add_fusion.10), channel_id=1, source_target_pairs={{0,2},{2,0},{1,3},{3,1},{4,6},{6,4},{5,7},{7,5},{8,10},{10,8},{9,1... | collective-permute-start | bytes 1843208 | tf_op jit(solution)/shard_map/ppermute | solution.py:66
  153.8 585.3 %reduce-scatter.15.cloned.1.call-start = ((), (), s32[]{:S(2)}) async-start(), calls=%async_computation.9 | async-start | bytes 3096576
  168.2 16.0 %collective-permute-start.5 = (f32[200,768]{1,0:T(8,128)S(1)}, f32[200,768]{1,0:T(8,128)}, u32[]{:S(2)}, u32[]{:S(2)}) collective-permute-start(f32[200,768]{1,0:T(8,128)S(1)} %add.1080), channel_id=1, source_target_pairs={{0,1},{1,0},{2,3},{3,2},{4,5},{5,4},{6,7},{7,6},{8,9},{9,8},{10,11... | collective-permute-start | bytes 1843208 | tf_op jit(solution)/shard_map/ppermute | solution.py:67
  181.3 4.1 collective-permute-start.17
  211.0 167.4 %copy-start.98 = (f32[400,192]{0,1:T(8,128)}, f32[400,192]{0,1:T(8,128)S(1)}, u32[]{:S(2)}) copy-start(f32[400,192]{0,1:T(8,128)S(1)} %reshape.2621) | copy-start | bytes 921604
  216.3 13.0 %collective-permute-start.6 = (f32[200,768]{1,0:T(8,128)}, f32[200,768]{1,0:T(8,128)}, u32[]{:S(2)}, u32[]{:S(2)}) collective-permute-start(f32[200,768]{1,0:T(8,128)} %slice_select_fusion.13), channel_id=1, source_target_pairs={{0,1},{1,0},{2,3},{3,2},{4,5},{5,4},{6,7},{7,6},{8,9},{9,8},{10,11... | collective-permute-start | bytes 1843208 | tf_op jit(solution)/shard_map/ppermute | solution.py:65
  224.9 170.2 %copy-start.100 = (f32[400,192]{0,1:T(8,128)}, f32[400,192]{0,1:T(8,128)S(1)}, u32[]{:S(2)}) copy-start(f32[400,192]{0,1:T(8,128)S(1)} %reshape.2631) | copy-start | bytes 921604
  228.3 4.8 collective-permute-start.18
  231.5 17.0 %collective-permute-start.7 = (f32[200,768]{1,0:T(8,128)}, f32[200,768]{1,0:T(8,128)}, u32[]{:S(2)}, u32[]{:S(2)}) collective-permute-start(f32[200,768]{1,0:T(8,128)} %select_add_fusion.13), channel_id=1, source_target_pairs={{0,2},{2,0},{1,3},{3,1},{4,6},{6,4},{5,7},{7,5},{8,10},{10,8},{9,1... | collective-permute-start | bytes 1843208 | tf_op jit(solution)/shard_map/ppermute | solution.py:66
  234.0 26.9 %collective-permute-start.19 = (f32[200,768]{1,0:T(8,128)}, f32[200,768]{1,0:T(8,128)}, u32[]{:S(2)}, u32[]{:S(2)}) collective-permute-start(f32[200,768]{1,0:T(8,128)} %select_add_fusion.9), channel_id=1, source_target_pairs={{0,2},{2,0},{1,3},{3,1},{4,6},{6,4},{5,7},{7,5},{8,10},{10,8},{9,1... | collective-permute-start | bytes 1843208 | tf_op jit(solution)/shard_map/ppermute | solution.py:66
  250.7 13.3 %collective-permute-start.8 = (f32[200,768]{1,0:T(8,128)}, f32[200,768]{1,0:T(8,128)}, u32[]{:S(2)}, u32[]{:S(2)}) collective-permute-start(f32[200,768]{1,0:T(8,128)} %add.1101), channel_id=1, source_target_pairs={{0,1},{1,0},{2,3},{3,2},{4,5},{5,4},{6,7},{7,6},{8,9},{9,8},{10,11... | collective-permute-start | bytes 1843208 | tf_op jit(solution)/shard_map/ppermute | solution.py:67
  262.2 4.2 collective-permute-start.20
  290.8 11.5 %collective-permute-start.24 = (f32[200,768]{1,0:T(8,128)S(1)}, f32[200,768]{1,0:T(8,128)S(1)}, u32[]{:S(2)}, u32[]{:S(2)}) collective-permute-start(f32[200,768]{1,0:T(8,128)S(1)} %slice_select_fusion.7), channel_id=1, source_target_pairs={{0,1},{1,0},{2,3},{3,2},{4,5},{5,4},{6,7},{7,6},{8,9},{9,8},{10,11... | collective-permute-start | bytes 1843208 | tf_op jit(solution)/shard_map/ppermute | solution.py:65
  296.6 7.1 collective-permute-start.36
  298.3 2.2 collective-permute-start.9
  300.5 5.7 collective-permute-start.21
  300.7 16.7 %collective-permute-start.10 = (f32[200,768]{1,0:T(8,128)S(1)}, f32[200,768]{1,0:T(8,128)S(1)}, u32[]{:S(2)}, u32[]{:S(2)}) collective-permute-start(f32[200,768]{1,0:T(8,128)S(1)} %select_add_fusion.12), channel_id=1, source_target_pairs={{0,2},{2,0},{1,3},{3,1},{4,6},{6,4},{5,7},{7,5},{8,10},{10,8},{9,1... | collective-permute-start | bytes 1843208 | tf_op jit(solution)/shard_map/ppermute | solution.py:66
  303.2 27.5 %collective-permute-start.25 = (f32[200,768]{1,0:T(8,128)}, f32[200,768]{1,0:T(8,128)}, u32[]{:S(2)}, u32[]{:S(2)}) collective-permute-start(f32[200,768]{1,0:T(8,128)} %select_add_fusion.7), channel_id=1, source_target_pairs={{0,2},{2,0},{1,3},{3,1},{4,6},{6,4},{5,7},{7,5},{8,10},{10,8},{9,1... | collective-permute-start | bytes 1843208 | tf_op jit(solution)/shard_map/ppermute | solution.py:66
  304.6 39.2 %collective-permute-start.37 = (f32[200,768]{1,0:T(8,128)}, f32[200,768]{1,0:T(8,128)}, u32[]{:S(2)}, u32[]{:S(2)}) collective-permute-start(f32[200,768]{1,0:T(8,128)} %select_add_fusion.3), channel_id=1, source_target_pairs={{0,2},{2,0},{1,3},{3,1},{4,6},{6,4},{5,7},{7,5},{8,10},{10,8},{9,1... | collective-permute-start | bytes 1843208 | tf_op jit(solution)/shard_map/ppermute | solution.py:66
  307.1 49.5 %collective-permute-start.22 = (f32[200,768]{1,0:T(8,128)}, f32[200,768]{1,0:T(8,128)}, u32[]{:S(2)}, u32[]{:S(2)}) collective-permute-start(f32[200,768]{1,0:T(8,128)} %select_add_fusion.8), channel_id=1, source_target_pairs={{0,2},{2,0},{1,3},{3,1},{4,6},{6,4},{5,7},{7,5},{8,10},{10,8},{9,1... | collective-permute-start | bytes 1843208 | tf_op jit(solution)/shard_map/ppermute | solution.py:66
  318.3 40.5 %collective-permute-start.11 = (f32[200,768]{1,0:T(8,128)}, f32[200,768]{1,0:T(8,128)}, u32[]{:S(2)}, u32[]{:S(2)}) collective-permute-start(f32[200,768]{1,0:T(8,128)} %add.1120), channel_id=1, source_target_pairs={{0,1},{1,0},{2,3},{3,2},{4,5},{5,4},{6,7},{7,6},{8,9},{9,8},{10,11... | collective-permute-start | bytes 1843208 | tf_op jit(solution)/shard_map/ppermute | solution.py:67
  332.0 28.2 %collective-permute-start.26 = (f32[200,768]{1,0:T(8,128)S(1)}, f32[200,768]{1,0:T(8,128)S(1)}, u32[]{:S(2)}, u32[]{:S(2)}) collective-permute-start(f32[200,768]{1,0:T(8,128)S(1)} %add.1175), channel_id=1, source_target_pairs={{0,1},{1,0},{2,3},{3,2},{4,5},{5,4},{6,7},{7,6},{8,9},{9,8},{10,11... | collective-permute-start | bytes 1843208 | tf_op jit(solution)/shard_map/ppermute | solution.py:67
  345.2 15.8 %collective-permute-start.38 = (f32[200,768]{1,0:T(8,128)S(1)}, f32[200,768]{1,0:T(8,128)S(1)}, u32[]{:S(2)}, u32[]{:S(2)}) collective-permute-start(f32[200,768]{1,0:T(8,128)S(1)} %add.1200), channel_id=1, source_target_pairs={{0,1},{1,0},{2,3},{3,2},{4,5},{5,4},{6,7},{7,6},{8,9},{9,8},{10,11... | collective-permute-start | bytes 1843208 | tf_op jit(solution)/shard_map/ppermute | solution.py:67
  358.8 93.9 %collective-permute-start.23 = (f32[200,768]{1,0:T(8,128)}, f32[200,768]{1,0:T(8,128)}, u32[]{:S(2)}, u32[]{:S(2)}) collective-permute-start(f32[200,768]{1,0:T(8,128)} %add.1168), channel_id=1, source_target_pairs={{0,1},{1,0},{2,3},{3,2},{4,5},{5,4},{6,7},{7,6},{8,9},{9,8},{10,11... | collective-permute-start | bytes 1843208 | tf_op jit(solution)/shard_map/ppermute | solution.py:67
  424.1 31.0 %collective-permute-start.27 = (f32[200,768]{1,0:T(8,128)}, f32[200,768]{1,0:T(8,128)}, u32[]{:S(2)}, u32[]{:S(2)}) collective-permute-start(f32[200,768]{1,0:T(8,128)} %slice_select_fusion.6), channel_id=1, source_target_pairs={{0,1},{1,0},{2,3},{3,2},{4,5},{5,4},{6,7},{7,6},{8,9},{9,8},{10,11... | collective-permute-start | bytes 1843208 | tf_op jit(solution)/shard_map/ppermute | solution.py:65
  446.5 12.4 %collective-permute-start.39 = (f32[200,768]{1,0:T(8,128)}, f32[200,768]{1,0:T(8,128)}, u32[]{:S(2)}, u32[]{:S(2)}) collective-permute-start(f32[200,768]{1,0:T(8,128)} %slice_select_fusion.2), channel_id=1, source_target_pairs={{0,1},{1,0},{2,3},{3,2},{4,5},{5,4},{6,7},{7,6},{8,9},{9,8},{10,11... | collective-permute-start | bytes 1843208 | tf_op jit(solution)/shard_map/ppermute | solution.py:65
  457.3 20.5 %collective-permute-start.28 = (f32[200,768]{1,0:T(8,128)}, f32[200,768]{1,0:T(8,128)}, u32[]{:S(2)}, u32[]{:S(2)}) collective-permute-start(f32[200,768]{1,0:T(8,128)} %select_add_fusion.6), channel_id=1, source_target_pairs={{0,2},{2,0},{1,3},{3,1},{4,6},{6,4},{5,7},{7,5},{8,10},{10,8},{9,1... | collective-permute-start | bytes 1843208 | tf_op jit(solution)/shard_map/ppermute | solution.py:66
  460.9 26.0 %collective-permute-start.40 = (f32[200,768]{1,0:T(8,128)}, f32[200,768]{1,0:T(8,128)}, u32[]{:S(2)}, u32[]{:S(2)}) collective-permute-start(f32[200,768]{1,0:T(8,128)} %select_add_fusion.2), channel_id=1, source_target_pairs={{0,2},{2,0},{1,3},{3,1},{4,6},{6,4},{5,7},{7,5},{8,10},{10,8},{9,1... | collective-permute-start | bytes 1843208 | tf_op jit(solution)/shard_map/ppermute | solution.py:66
  479.2 12.2 %collective-permute-start.29 = (f32[200,768]{1,0:T(8,128)S(1)}, f32[200,768]{1,0:T(8,128)S(1)}, u32[]{:S(2)}, u32[]{:S(2)}) collective-permute-start(f32[200,768]{1,0:T(8,128)S(1)} %add.1181), channel_id=1, source_target_pairs={{0,1},{1,0},{2,3},{3,2},{4,5},{5,4},{6,7},{7,6},{8,9},{9,8},{10,11... | collective-permute-start | bytes 1843208 | tf_op jit(solution)/shard_map/ppermute | solution.py:67
  488.2 3.3 collective-permute-start.41
  522.9 219.6 %reduce-scatter.19.cloned.1.call-start = ((), (), s32[]{:S(2)}) async-start(), calls=%async_computation.11 | async-start | bytes 5308416
  532.5 8.5 collective-permute-start.30
  537.1 5.7 collective-permute-start.42
  541.1 16.8 %collective-permute-start.31 = (f32[200,768]{1,0:T(8,128)S(1)}, f32[200,768]{1,0:T(8,128)S(1)}, u32[]{:S(2)}, u32[]{:S(2)}) collective-permute-start(f32[200,768]{1,0:T(8,128)S(1)} %select_add_fusion.5), channel_id=1, source_target_pairs={{0,2},{2,0},{1,3},{3,1},{4,6},{6,4},{5,7},{7,5},{8,10},{10,8},{9,1... | collective-permute-start | bytes 1843208 | tf_op jit(solution)/shard_map/ppermute | solution.py:66
  542.9 27.3 %collective-permute-start.43 = (f32[200,768]{1,0:T(8,128)S(1)}, f32[200,768]{1,0:T(8,128)S(1)}, u32[]{:S(2)}, u32[]{:S(2)}) collective-permute-start(f32[200,768]{1,0:T(8,128)S(1)} %select_add_fusion.1), channel_id=1, source_target_pairs={{0,2},{2,0},{1,3},{3,1},{4,6},{6,4},{5,7},{7,5},{8,10},{10,8},{9,1... | collective-permute-start | bytes 1843208 | tf_op jit(solution)/shard_map/ppermute | solution.py:66
  558.0 21.5 %collective-permute-start.32 = (f32[200,768]{1,0:T(8,128)S(1)}, f32[200,768]{1,0:T(8,128)S(1)}, u32[]{:S(2)}, u32[]{:S(2)}) collective-permute-start(f32[200,768]{1,0:T(8,128)S(1)} %add.1188), channel_id=1, source_target_pairs={{0,1},{1,0},{2,3},{3,2},{4,5},{5,4},{6,7},{7,6},{8,9},{9,8},{10,11... | collective-permute-start | bytes 1843208 | tf_op jit(solution)/shard_map/ppermute | solution.py:67
  570.3 9.4 %collective-permute-start.44 = (f32[200,768]{1,0:T(8,128)S(1)}, f32[200,768]{1,0:T(8,128)S(1)}, u32[]{:S(2)}, u32[]{:S(2)}) collective-permute-start(f32[200,768]{1,0:T(8,128)S(1)} %add.1213), channel_id=1, source_target_pairs={{0,1},{1,0},{2,3},{3,2},{4,5},{5,4},{6,7},{7,6},{8,9},{9,8},{10,11... | collective-permute-start | bytes 1843208 | tf_op jit(solution)/shard_map/ppermute | solution.py:67
  579.3 197.4 %reduce-scatter.13.cloned.1.call-start = ((), (), s32[]{:S(2)}) async-start(), calls=%async_computation.8 | async-start | bytes 3096576
  617.1 42.2 %collective-permute-start.33 = (f32[200,768]{1,0:T(8,128)}, f32[200,768]{1,0:T(8,128)}, u32[]{:S(2)}, u32[]{:S(2)}) collective-permute-start(f32[200,768]{1,0:T(8,128)} %slice_select_fusion.4), channel_id=1, source_target_pairs={{0,1},{1,0},{2,3},{3,2},{4,5},{5,4},{6,7},{7,6},{8,9},{9,8},{10,11... | collective-permute-start | bytes 1843208 | tf_op jit(solution)/shard_map/ppermute | solution.py:65
  649.8 13.2 %collective-permute-start.45 = (f32[200,768]{1,0:T(8,128)}, f32[200,768]{1,0:T(8,128)}, u32[]{:S(2)}, u32[]{:S(2)}) collective-permute-start(f32[200,768]{1,0:T(8,128)} %slice_select_fusion), channel_id=1, source_target_pairs={{0,1},{1,0},{2,3},{3,2},{4,5},{5,4},{6,7},{7,6},{8,9},{9,8},{10,11... | collective-permute-start | bytes 1843208 | tf_op jit(solution)/shard_map/ppermute | solution.py:65
  661.4 17.0 %collective-permute-start.34 = (f32[200,768]{1,0:T(8,128)}, f32[200,768]{1,0:T(8,128)}, u32[]{:S(2)}, u32[]{:S(2)}) collective-permute-start(f32[200,768]{1,0:T(8,128)} %select_add_fusion.4), channel_id=1, source_target_pairs={{0,2},{2,0},{1,3},{3,1},{4,6},{6,4},{5,7},{7,5},{8,10},{10,8},{9,1... | collective-permute-start | bytes 1843208 | tf_op jit(solution)/shard_map/ppermute | solution.py:66
  665.0 25.9 %collective-permute-start.46 = (f32[200,768]{1,0:T(8,128)}, f32[200,768]{1,0:T(8,128)}, u32[]{:S(2)}, u32[]{:S(2)}) collective-permute-start(f32[200,768]{1,0:T(8,128)} %select_add_fusion), channel_id=1, source_target_pairs={{0,2},{2,0},{1,3},{3,1},{4,6},{6,4},{5,7},{7,5},{8,10},{10,8},{9,1... | collective-permute-start | bytes 1843208 | tf_op jit(solution)/shard_map/ppermute | solution.py:66
  679.8 15.7 %collective-permute-start.35 = (f32[200,768]{1,0:T(8,128)S(1)}, f32[200,768]{1,0:T(8,128)S(1)}, u32[]{:S(2)}, u32[]{:S(2)}) collective-permute-start(f32[200,768]{1,0:T(8,128)S(1)} %add.1194), channel_id=1, source_target_pairs={{0,1},{1,0},{2,3},{3,2},{4,5},{5,4},{6,7},{7,6},{8,9},{9,8},{10,11... | collective-permute-start | bytes 1843208 | tf_op jit(solution)/shard_map/ppermute | solution.py:67
  692.3 3.3 collective-permute-start.47
  706.8 168.0 %reduce-scatter.17.cloned.1.call-start = ((), (), s32[]{:S(2)}) async-start(), calls=%async_computation.10 | async-start | bytes 5308416
  743.7 35.3 %slice-start = ((f32[4,2,3,8]{3,2,1,0:T(4,128)}), f32[1,2,3,8]{3,2,1,0:T(4,128)S(1)}, s32[]{:S(2)}) async-start(f32[4,2,3,8]{3,2,1,0:T(4,128)} %copy-done.221), calls=%async_computation.12 | async-start | bytes 8192 | tf_op jit(solution)/shard_map/slice | solution.py:275
  (260 other events, 693.3 us)
Sparse Core Ops, SparseCore 0:
  13.7 44.9 all-gather.4
  60.9 50.6 all-gather.6
  122.8 41.3 all-gather.8
  166.2 50.6 all-gather.10
  523.0 69.7 reduce-scatter.14
  596.3 94.3 reduce-scatter.18
  706.9 69.7 reduce-scatter.12
  780.3 94.4 reduce-scatter.16
where the time goes:
time: 901 us; the launch traced here: 886 us
  waiting for transfers between devices  303 us (34%)
  local copies, waits for them, and re-layouts  216 us (24%)
  other arithmetic  172 us (19%)
  matrix products  151 us (17%)
  starting transfers between devices  23.9 us (3%)
  between operations  19 us (2%)
    ppermute x16, waiting for transfers between devices, tensor_sum(): mine = mine + lax.ppermute(mine, 'tensor', chip_pairs)  142 us
    unnamed x12, waiting for transfers between devices  123 us
    unnamed x563, local copies, waits for them, and re-layouts  81.2 us
    dot_general x16, matrix products, cross(): lax.dot_general(a, b, (((0,), (0,)), ((), ())), precision=high, preferred...  41.3 us
    dot_general x24, matrix products, heads_product(): return jnp.einsum(spec, a, b, precision=high, preferred_element_type=f32)  40.3 us
    all_gather x2, waiting for transfers between devices, gather_weights(): attention = lax.all_gather(attention, 'dp', axis=0, tiled=True)  37.4 us
    dot_general x32, matrix products, weight_product(): lax.dot_general(top.astype(bf16), w, dims, preferred_element_type=f32)  36.3 us
    dot_general x32, matrix products, weight_product(): lax.dot_general(rest, w, dims, preferred_element_type=f32)  33.5 us
  transfers between devices with their start and end apart: 56, of which 18 were waited for; matrix products, arithmetic and copies ran while one was open for 50% of the time, Pallas kernels for 0%

commit v1 on v0

--- a/solution.py
+++ b/solution.py
@@ -86,8 +86,11 @@
         [qkv.reshape(depth, 3 * inner), out.reshape(inner, depth).T, small], axis=1
     )
     feed = jnp.concatenate([up, down.T], axis=1)
-    attention = lax.all_gather(attention, "dp", axis=0, tiled=True)
-    feed = lax.all_gather(feed, "dp", axis=0, tiled=True)
+    attention, feed = jnp.split(
+        lax.all_gather(jnp.concatenate([attention, feed], axis=1), "dp", axis=0, tiled=True),
+        [attention.shape[1]],
+        axis=1,
+    )
     width = attention.shape[0]
     n = width // depth
     small = attention[:, 4 * inner :].astype(f32).T

time: 901 us -> 938 us (1.041)
  waiting for transfers between devices: 303 us -> 370 us
  local copies, waits for them, and re-layouts: 216 us -> 188 us
  matrix products: 151 us -> 170 us
  other arithmetic: 172 us -> 153 us
    all_gather x4 -> x2, waiting for transfers between devices: 37.4 us -> 85.6 us  [gather_weights(): lax.all_gather(jnp.concatenate([attention, feed], axis=1), 'dp', axis=0,...]
    ppermute x16, waiting for transfers between devices: 142 us -> 161 us  [tensor_sum(): mine = mine + lax.ppermute(mine, 'tensor', chip_pairs)]
    dot_general x32, matrix products: 33.5 us -> 45.5 us  [weight_product(): lax.dot_general(rest, w, dims, preferred_element_type=f32)]
    dot_general x32, matrix products: 36.3 us -> 47 us  [weight_product(): lax.dot_general(top.astype(bf16), w, dims, preferred_element_type=f32)]
    reduce_sum x4, other arithmetic: 1.57 us -> 11.9 us  [layer_forward(): soft = exponent / jnp.sum(exponent, axis=-1, keepdims=True)]
    unnamed x563 -> x447, local copies, waits for them, and re-layouts: 81.2 us -> 80.6 us
    unnamed x12 -> x10, waiting for transfers between devices: 123 us -> 123 us
  transfers between devices with their start and end apart: 56 -> 54, of which waited for: 18 -> 19; matrix products, arithmetic and copies ran while one was open for 50% -> 42% of each run, Pallas kernels for 0% -> 0%
where the time goes in v1:
time: 938 us; the launch traced here: 924 us
  waiting for transfers between devices  370 us (39%)
  local copies, waits for them, and re-layouts  188 us (20%)
  matrix products  170 us (18%)
  other arithmetic  153 us (16%)
  starting transfers between devices  24.5 us (3%)
  between operations  18.6 us (2%)
    ppermute x16, waiting for transfers between devices, tensor_sum(): mine = mine + lax.ppermute(mine, 'tensor', chip_pairs)  161 us
    unnamed x10, waiting for transfers between devices  123 us
    all_gather x2, waiting for transfers between devices, gather_weights(): lax.all_gather(jnp.concatenate([attention, feed], axis=1), 'dp', axis=0,...  85.6 us
    unnamed x447, local copies, waits for them, and re-layouts  80.6 us
    dot_general x32, matrix products, weight_product(): lax.dot_general(top.astype(bf16), w, dims, preferred_element_type=f32)  47 us
    dot_general x32, matrix products, weight_product(): lax.dot_general(rest, w, dims, preferred_element_type=f32)  45.5 us
    dot_general x16, matrix products, cross(): lax.dot_general(a, b, (((0,), (0,)), ((), ())), precision=high, preferred...  40.2 us
    dot_general x24, matrix products, heads_product(): return jnp.einsum(spec, a, b, precision=high, preferred_element_type=f32)  37.5 us
  transfers between devices with their start and end apart: 54, of which 19 were waited for; matrix products, arithmetic and copies ran while one was open for 42% of the time, Pallas kernels for 0%

profile of v1, /device:TPU:0, one launch (start us, length us, event | category | flops | bytes accessed | tf_op | source)
XLA Modules:
  0.0 923.7 jit_solution(1288500887888562045)
XLA Ops:
  23.1 64.3 %all-gather.3.cloned.1.call-done = bf16[768,2432]{1,0:T(8,128)(2,1)} async-done(((bf16[96,2432]{1,0:T(8,128)(2,1)}), bf16[768,2432]{1,0:T(8,128)(2,1)}) %all-gather.3.cloned.1.call-update) | async-done | bytes 3735568 | tf_op jit(solution)/shard_map/all_gather | solution.py:90
  115.4 11.3 %fusion.78 = f32[2,3,200]{2,1,0:T(4,128)S(1)} fusion(f32[2,3,200,200]{2,3,1,0:T(8,128)S(1)} %get-tuple-element.293, f32[2,3,200]{2,1,0:T(4,128)S(1)} %get-tuple-element.292), kind=kLoop, calls=%fused_computation.312 | loop fusion | flops 478800 | bytes 969600 | tf_op jit(solution)/shard_map/reduce_sum | solution.py:139
  136.1 14.4 %collective-permute-done.1 = f32[200,768]{1,0:T(8,128)S(1)} collective-permute-done((f32[200,768]{1,0:T(8,128)S(1)}, f32[200,768]{1,0:T(8,128)S(1)}, u32[]{:S(2)}, u32[]{:S(2)}) %collective-permute-start.1) | collective-permute-done | bytes 614432 | tf_op jit(solution)/shard_map/ppermute | solution.py:66
  150.7 12.6 %collective-permute-done.13 = f32[200,768]{1,0:T(8,128)S(1)} collective-permute-done((f32[200,768]{1,0:T(8,128)S(1)}, f32[200,768]{1,0:T(8,128)S(1)}, u32[]{:S(2)}, u32[]{:S(2)}) %collective-permute-start.13) | collective-permute-done | bytes 614432 | tf_op jit(solution)/shard_map/ppermute | solution.py:66
  187.3 2.6 fusion.118
  190.2 3.3 fusion.338
  199.3 14.1 %collective-permute-done.4 = f32[200,768]{1,0:T(8,128)S(1)} collective-permute-done((f32[200,768]{1,0:T(8,128)S(1)}, f32[200,768]{1,0:T(8,128)S(1)}, u32[]{:S(2)}, u32[]{:S(2)}) %collective-permute-start.4) | collective-permute-done | bytes 614432 | tf_op jit(solution)/shard_map/ppermute | solution.py:66
  213.5 21.3 %all-gather.5.cloned.1.call-done = bf16[768,2432]{1,0:T(8,128)(2,1)} async-done(((bf16[96,2432]{1,0:T(8,128)(2,1)}), bf16[768,2432]{1,0:T(8,128)(2,1)}) %all-gather.5.cloned.1.call-update) | async-done | bytes 3735568 | tf_op jit(solution)/shard_map/all_gather | solution.py:90
  246.2 2.5 fusion.120
  249.0 2.6 convolution_add_fusion.24
  281.7 11.6 %collective-permute-done.7 = f32[200,768]{1,0:T(8,128)} collective-permute-done((f32[200,768]{1,0:T(8,128)}, f32[200,768]{1,0:T(8,128)}, u32[]{:S(2)}, u32[]{:S(2)}) %collective-permute-start.7) | collective-permute-done | bytes 614432 | tf_op jit(solution)/shard_map/ppermute | solution.py:66
  294.8 3.1 fusion.123
  297.9 8.2 collective-permute-done.19
  307.6 3.0 fusion.129
  319.0 2.9 subtract_multiply_fusion.3
  344.5 9.8 %collective-permute-done.10 = f32[200,768]{1,0:T(8,128)S(1)} collective-permute-done((f32[200,768]{1,0:T(8,128)S(1)}, f32[200,768]{1,0:T(8,128)S(1)}, u32[]{:S(2)}, u32[]{:S(2)}) %collective-permute-start.10) | collective-permute-done | bytes 614432 | tf_op jit(solution)/shard_map/ppermute | solution.py:66
  355.4 12.2 %collective-permute-done.25 = f32[200,768]{1,0:T(8,128)} collective-permute-done((f32[200,768]{1,0:T(8,128)}, f32[200,768]{1,0:T(8,128)}, u32[]{:S(2)}, u32[]{:S(2)}) %collective-permute-start.25) | collective-permute-done | bytes 614432 | tf_op jit(solution)/shard_map/ppermute | solution.py:66
  369.0 5.1 fusion.82
  374.1 6.7 collective-permute-done.37
  382.1 11.3 %collective-permute-done.22 = f32[200,768]{1,0:T(8,128)} collective-permute-done((f32[200,768]{1,0:T(8,128)}, f32[200,768]{1,0:T(8,128)}, u32[]{:S(2)}, u32[]{:S(2)}) %collective-permute-start.22) | collective-permute-done | bytes 614432 | tf_op jit(solution)/shard_map/ppermute | solution.py:66
  402.8 4.8 multiply_add_fusion.12
  409.6 2.5 fusion.378
  417.5 2.4 fusion.16
  425.9 2.5 fusion.379
  431.6 2.5 reshape.2644
  434.1 2.4 fusion.14
  487.8 2.5 broadcast_select_fusion.17
  497.0 2.5 pad_maximum_fusion.9
  499.5 9.9 %collective-permute-done.28 = f32[200,768]{1,0:T(8,128)} collective-permute-done((f32[200,768]{1,0:T(8,128)}, f32[200,768]{1,0:T(8,128)}, u32[]{:S(2)}, u32[]{:S(2)}) %collective-permute-start.28) | collective-permute-done | bytes 614432 | tf_op jit(solution)/shard_map/ppermute | solution.py:66
  510.9 3.2 fusion.84
  514.1 7.9 collective-permute-done.40
  523.4 3.1 fusion.86
  531.5 3.9 fusion.328
  536.8 4.5 fusion.341
  545.1 3.2 maximum_add_fusion.3
  554.1 3.3 multiply_add_fusion.10
  568.4 2.6 fusion.81
  573.4 2.5 fusion.319
  576.0 11.9 %collective-permute-done.31 = f32[200,768]{1,0:T(8,128)S(1)} collective-permute-done((f32[200,768]{1,0:T(8,128)S(1)}, f32[200,768]{1,0:T(8,128)S(1)}, u32[]{:S(2)}, u32[]{:S(2)}) %collective-permute-start.31) | collective-permute-done | bytes 614432 | tf_op jit(solution)/shard_map/ppermute | solution.py:66
  588.1 2.7 fusion.323
  590.9 9.3 %collective-permute-done.43 = f32[200,768]{1,0:T(8,128)S(1)} collective-permute-done((f32[200,768]{1,0:T(8,128)S(1)}, f32[200,768]{1,0:T(8,128)S(1)}, u32[]{:S(2)}, u32[]{:S(2)}) %collective-permute-start.43) | collective-permute-done | bytes 614432 | tf_op jit(solution)/shard_map/ppermute | solution.py:66
  600.3 2.7 maximum_add_fusion.1
  603.0 6.1 copy.588
  614.0 4.4 multiply_add_fusion.8
  626.8 2.4 fusion.15
  645.8 2.4 fusion.200
  653.9 2.5 fusion.381
  661.8 2.5 fusion.13
  669.0 2.5 convolution_bitcast_fusion.1
  689.5 3.9 fusion.344
  693.5 4.5 fusion.394
  706.3 10.9 %collective-permute-done.34 = f32[200,768]{1,0:T(8,128)} collective-permute-done((f32[200,768]{1,0:T(8,128)}, f32[200,768]{1,0:T(8,128)}, u32[]{:S(2)}, u32[]{:S(2)}) %collective-permute-start.34) | collective-permute-done | bytes 614432 | tf_op jit(solution)/shard_map/ppermute | solution.py:66
  719.3 10.1 %collective-permute-done.46 = f32[200,768]{1,0:T(8,128)} collective-permute-done((f32[200,768]{1,0:T(8,128)}, f32[200,768]{1,0:T(8,128)}, u32[]{:S(2)}, u32[]{:S(2)}) %collective-permute-start.46) | collective-permute-done | bytes 614432 | tf_op jit(solution)/shard_map/ppermute | solution.py:66
  738.4 3.4 select_maximum_fusion.1
  741.7 3.3 copy.582
  745.3 4.3 fusion.400
  749.7 2.6 fusion.401
  752.3 2.7 fusion.85
  755.1 2.7 fusion.83
  757.8 2.7 maximum_add_fusion
  760.5 6.3 copy.586
  771.9 2.9 multiply_add_fusion.7
  782.3 32.7 %reduce-scatter.13.cloned.1.call-done = f32[96,896]{1,0:T(8,128)} async-done(((f32[768,896]{1,0:T(8,128)}), f32[96,896]{1,0:T(8,128)}) %reduce-scatter.13.cloned.1.call-update) | async-done | bytes 344080
  822.4 90.6 %reduce-scatter.17.cloned.1.call-done = f32[96,1536]{1,0:T(8,128)} async-done(((f32[768,1536]{1,0:T(8,128)}), f32[96,1536]{1,0:T(8,128)}) %reduce-scatter.17.cloned.1.call-update) | async-done | bytes 589840
  (991 shorter events, 383.1 us)
Async XLA Ops:
  7.2 80.2 %all-gather.3.cloned.1.call-start = ((), (), s32[]{:S(2)}) async-start(), calls=%async_computation.4 | async-start | bytes 4202496 | tf_op jit(solution)/shard_map/all_gather | solution.py:90
  16.9 218.0 %all-gather.5.cloned.1.call-start = ((), (), s32[]{:S(2)}) async-start(), calls=%async_computation.5 | async-start | bytes 4202496 | tf_op jit(solution)/shard_map/all_gather | solution.py:90
  19.1 155.5 %copy-start.4 = (f32[4,197,768]{2,1,0:T(8,128)}, f32[4,197,768]{2,1,0:T(8,128)S(1)}, u32[]{:S(2)}) copy-start(f32[4,197,768]{2,1,0:T(8,128)S(1)} %copy.444) | copy-start | bytes 7262212
  22.4 65.9 %copy-start.175 = (f32[2,200]{1,0:T(2,128)}, f32[2,200]{1,0:T(2,128)S(1)}, u32[]{:S(2)}) copy-start(f32[2,200]{1,0:T(2,128)S(1)} %add_rsqrt_fusion.3) | copy-start | bytes 4804
  89.5 100.4 %copy-start.161 = (f32[768]{0:T(1024)}, f32[768]{0:T(1024)S(1)}, u32[]{:S(2)}) copy-start(f32[768]{0:T(1024)S(1)} %get-tuple-element.90) | copy-start | bytes 9220
  89.5 100.4 %copy-start.173 = (f32[768]{0:T(1024)}, f32[768]{0:T(1024)S(1)}, u32[]{:S(2)}) copy-start(f32[768]{0:T(1024)S(1)} %get-tuple-element.89) | copy-start | bytes 9220
  109.8 22.1 %collective-permute-start = (f32[200,768]{1,0:T(8,128)}, f32[200,768]{1,0:T(8,128)}, u32[]{:S(2)}, u32[]{:S(2)}) collective-permute-start(f32[200,768]{1,0:T(8,128)} %slice_select_fusion.15), channel_id=1, source_target_pairs={{0,1},{1,0},{2,3},{3,2},{4,5},{5,4},{6,7},{7,6},{8,9},{9,8},{10,11... | collective-permute-start | bytes 1843208 | tf_op jit(solution)/shard_map/ppermute | solution.py:65
  131.4 3.9 collective-permute-start.12
  133.7 16.7 %collective-permute-start.1 = (f32[200,768]{1,0:T(8,128)S(1)}, f32[200,768]{1,0:T(8,128)S(1)}, u32[]{:S(2)}, u32[]{:S(2)}) collective-permute-start(f32[200,768]{1,0:T(8,128)S(1)} %select_add_fusion.15), channel_id=1, source_target_pairs={{0,2},{2,0},{1,3},{3,1},{4,6},{6,4},{5,7},{7,5},{8,10},{10,8},{9,1... | collective-permute-start | bytes 1843208 | tf_op jit(solution)/shard_map/ppermute | solution.py:66
  135.4 27.8 %collective-permute-start.13 = (f32[200,768]{1,0:T(8,128)S(1)}, f32[200,768]{1,0:T(8,128)S(1)}, u32[]{:S(2)}, u32[]{:S(2)}) collective-permute-start(f32[200,768]{1,0:T(8,128)S(1)} %select_add_fusion.11), channel_id=1, source_target_pairs={{0,2},{2,0},{1,3},{3,1},{4,6},{6,4},{5,7},{7,5},{8,10},{10,8},{9,1... | collective-permute-start | bytes 1843208 | tf_op jit(solution)/shard_map/ppermute | solution.py:66
  150.6 16.1 %copy-start.153 = (bf16[96,768]{1,0:T(8,128)(2,1)S(1)}, bf16[96,768]{1,0:T(8,128)(2,1)}, u32[]{:S(2)}) copy-start(bf16[96,768]{1,0:T(8,128)(2,1)} %get-tuple-element.237) | copy-start | bytes 442372
  150.6 18.8 %collective-permute-start.2 = (f32[200,768]{1,0:T(8,128)S(1)}, f32[200,768]{1,0:T(8,128)}, u32[]{:S(2)}, u32[]{:S(2)}) collective-permute-start(f32[200,768]{1,0:T(8,128)S(1)} %add.1061), channel_id=1, source_target_pairs={{0,1},{1,0},{2,3},{3,2},{4,5},{5,4},{6,7},{7,6},{8,9},{9,8},{10,11... | collective-permute-start | bytes 1843208 | tf_op jit(solution)/shard_map/ppermute | solution.py:67
  164.2 6.5 collective-permute-start.14
  168.4 608.9 %reduce-scatter.15.cloned.1.call-start = ((), (), s32[]{:S(2)}) async-start(), calls=%async_computation.7 | async-start | bytes 3096576
  186.3 9.6 %collective-permute-start.3 = (f32[200,768]{1,0:T(8,128)}, f32[200,768]{1,0:T(8,128)S(1)}, u32[]{:S(2)}, u32[]{:S(2)}) collective-permute-start(f32[200,768]{1,0:T(8,128)} %slice_select_fusion.14), channel_id=1, source_target_pairs={{0,1},{1,0},{2,3},{3,2},{4,5},{5,4},{6,7},{7,6},{8,9},{9,8},{10,11... | collective-permute-start | bytes 1843208 | tf_op jit(solution)/shard_map/ppermute | solution.py:65
  195.3 2.8 collective-permute-start.15
  196.6 16.7 %collective-permute-start.4 = (f32[200,768]{1,0:T(8,128)S(1)}, f32[200,768]{1,0:T(8,128)S(1)}, u32[]{:S(2)}, u32[]{:S(2)}) collective-permute-start(f32[200,768]{1,0:T(8,128)S(1)} %select_add_fusion.14), channel_id=1, source_target_pairs={{0,2},{2,0},{1,3},{3,1},{4,6},{6,4},{5,7},{7,5},{8,10},{10,8},{9,1... | collective-permute-start | bytes 1843208 | tf_op jit(solution)/shard_map/ppermute | solution.py:66
  198.3 37.6 %copy-start.141 = (f32[200,768]{1,0:T(8,128)}, f32[200,768]{1,0:T(8,128)S(1)}, u32[]{:S(2)}) copy-start(f32[200,768]{1,0:T(8,128)S(1)} %select_add_fusion.10) | copy-start | bytes 1843204
  198.4 37.9 %collective-permute-start.16 = (f32[200,768]{1,0:T(8,128)S(1)}, f32[200,768]{1,0:T(8,128)}, u32[]{:S(2)}, u32[]{:S(2)}) collective-permute-start(f32[200,768]{1,0:T(8,128)S(1)} %select_add_fusion.10), channel_id=1, source_target_pairs={{0,2},{2,0},{1,3},{3,1},{4,6},{6,4},{5,7},{7,5},{8,10},{10,8},{9,1... | collective-permute-start | bytes 1843208 | tf_op jit(solution)/shard_map/ppermute | solution.py:66
  213.4 25.7 %collective-permute-start.5 = (f32[200,768]{1,0:T(8,128)S(1)}, f32[200,768]{1,0:T(8,128)}, u32[]{:S(2)}, u32[]{:S(2)}) collective-permute-start(f32[200,768]{1,0:T(8,128)S(1)} %add.1080), channel_id=1, source_target_pairs={{0,1},{1,0},{2,3},{3,2},{4,5},{5,4},{6,7},{7,6},{8,9},{9,8},{10,11... | collective-permute-start | bytes 1843208 | tf_op jit(solution)/shard_map/ppermute | solution.py:67
  237.6 2.7 collective-permute-start.17
  262.1 12.4 %collective-permute-start.6 = (f32[200,768]{1,0:T(8,128)}, f32[200,768]{1,0:T(8,128)}, u32[]{:S(2)}, u32[]{:S(2)}) collective-permute-start(f32[200,768]{1,0:T(8,128)} %slice_select_fusion.13), channel_id=1, source_target_pairs={{0,1},{1,0},{2,3},{3,2},{4,5},{5,4},{6,7},{7,6},{8,9},{9,8},{10,11... | collective-permute-start | bytes 1843208 | tf_op jit(solution)/shard_map/ppermute | solution.py:65
  273.6 4.2 collective-permute-start.18
  276.4 17.0 %collective-permute-start.7 = (f32[200,768]{1,0:T(8,128)}, f32[200,768]{1,0:T(8,128)}, u32[]{:S(2)}, u32[]{:S(2)}) collective-permute-start(f32[200,768]{1,0:T(8,128)} %select_add_fusion.13), channel_id=1, source_target_pairs={{0,2},{2,0},{1,3},{3,1},{4,6},{6,4},{5,7},{7,5},{8,10},{10,8},{9,1... | collective-permute-start | bytes 1843208 | tf_op jit(solution)/shard_map/ppermute | solution.py:66
  278.8 27.3 %collective-permute-start.19 = (f32[200,768]{1,0:T(8,128)}, f32[200,768]{1,0:T(8,128)}, u32[]{:S(2)}, u32[]{:S(2)}) collective-permute-start(f32[200,768]{1,0:T(8,128)} %select_add_fusion.9), channel_id=1, source_target_pairs={{0,2},{2,0},{1,3},{3,1},{4,6},{6,4},{5,7},{7,5},{8,10},{10,8},{9,1... | collective-permute-start | bytes 1843208 | tf_op jit(solution)/shard_map/ppermute | solution.py:66
  294.7 15.8 %collective-permute-start.8 = (f32[200,768]{1,0:T(8,128)S(1)}, f32[200,768]{1,0:T(8,128)S(1)}, u32[]{:S(2)}, u32[]{:S(2)}) collective-permute-start(f32[200,768]{1,0:T(8,128)S(1)} %add.1101), channel_id=1, source_target_pairs={{0,1},{1,0},{2,3},{3,2},{4,5},{5,4},{6,7},{7,6},{8,9},{9,8},{10,11... | collective-permute-start | bytes 1843208 | tf_op jit(solution)/shard_map/ppermute | solution.py:67
  307.5 4.2 collective-permute-start.20
  327.7 11.4 %collective-permute-start.24 = (f32[200,768]{1,0:T(8,128)S(1)}, f32[200,768]{1,0:T(8,128)S(1)}, u32[]{:S(2)}, u32[]{:S(2)}) collective-permute-start(f32[200,768]{1,0:T(8,128)S(1)} %slice_select_fusion.7), channel_id=1, source_target_pairs={{0,1},{1,0},{2,3},{3,2},{4,5},{5,4},{6,7},{7,6},{8,9},{9,8},{10,11... | collective-permute-start | bytes 1843208 | tf_op jit(solution)/shard_map/ppermute | solution.py:65
  333.3 7.3 collective-permute-start.36
  335.0 2.4 collective-permute-start.9
  337.4 5.7 collective-permute-start.21
  337.6 16.7 %collective-permute-start.10 = (f32[200,768]{1,0:T(8,128)S(1)}, f32[200,768]{1,0:T(8,128)S(1)}, u32[]{:S(2)}, u32[]{:S(2)}) collective-permute-start(f32[200,768]{1,0:T(8,128)S(1)} %select_add_fusion.12), channel_id=1, source_target_pairs={{0,2},{2,0},{1,3},{3,1},{4,6},{6,4},{5,7},{7,5},{8,10},{10,8},{9,1... | collective-permute-start | bytes 1843208 | tf_op jit(solution)/shard_map/ppermute | solution.py:66
  340.0 27.5 %collective-permute-start.25 = (f32[200,768]{1,0:T(8,128)}, f32[200,768]{1,0:T(8,128)}, u32[]{:S(2)}, u32[]{:S(2)}) collective-permute-start(f32[200,768]{1,0:T(8,128)} %select_add_fusion.7), channel_id=1, source_target_pairs={{0,2},{2,0},{1,3},{3,1},{4,6},{6,4},{5,7},{7,5},{8,10},{10,8},{9,1... | collective-permute-start | bytes 1843208 | tf_op jit(solution)/shard_map/ppermute | solution.py:66
  341.6 39.2 %collective-permute-start.37 = (f32[200,768]{1,0:T(8,128)}, f32[200,768]{1,0:T(8,128)}, u32[]{:S(2)}, u32[]{:S(2)}) collective-permute-start(f32[200,768]{1,0:T(8,128)} %select_add_fusion.3), channel_id=1, source_target_pairs={{0,2},{2,0},{1,3},{3,1},{4,6},{6,4},{5,7},{7,5},{8,10},{10,8},{9,1... | collective-permute-start | bytes 1843208 | tf_op jit(solution)/shard_map/ppermute | solution.py:66
  344.0 49.5 %collective-permute-start.22 = (f32[200,768]{1,0:T(8,128)}, f32[200,768]{1,0:T(8,128)}, u32[]{:S(2)}, u32[]{:S(2)}) collective-permute-start(f32[200,768]{1,0:T(8,128)} %select_add_fusion.8), channel_id=1, source_target_pairs={{0,2},{2,0},{1,3},{3,1},{4,6},{6,4},{5,7},{7,5},{8,10},{10,8},{9,1... | collective-permute-start | bytes 1843208 | tf_op jit(solution)/shard_map/ppermute | solution.py:66
  355.2 40.4 %collective-permute-start.11 = (f32[200,768]{1,0:T(8,128)}, f32[200,768]{1,0:T(8,128)}, u32[]{:S(2)}, u32[]{:S(2)}) collective-permute-start(f32[200,768]{1,0:T(8,128)} %add.1120), channel_id=1, source_target_pairs={{0,1},{1,0},{2,3},{3,2},{4,5},{5,4},{6,7},{7,6},{8,9},{9,8},{10,11... | collective-permute-start | bytes 1843208 | tf_op jit(solution)/shard_map/ppermute | solution.py:67
  355.4 13.6 %copy-start.41 = (f32[400,768]{1,0:T(8,128)S(1)}, f32[400,768]{1,0:T(8,128)}, u32[]{:S(2)}) copy-start(f32[400,768]{1,0:T(8,128)} %copy-done.40) | copy-start | bytes 3686404
  368.9 28.2 %collective-permute-start.26 = (f32[200,768]{1,0:T(8,128)S(1)}, f32[200,768]{1,0:T(8,128)S(1)}, u32[]{:S(2)}, u32[]{:S(2)}) collective-permute-start(f32[200,768]{1,0:T(8,128)S(1)} %add.1175), channel_id=1, source_target_pairs={{0,1},{1,0},{2,3},{3,2},{4,5},{5,4},{6,7},{7,6},{8,9},{9,8},{10,11... | collective-permute-start | bytes 1843208 | tf_op jit(solution)/shard_map/ppermute | solution.py:67
  382.0 15.2 %collective-permute-start.38 = (f32[200,768]{1,0:T(8,128)S(1)}, f32[200,768]{1,0:T(8,128)S(1)}, u32[]{:S(2)}, u32[]{:S(2)}) collective-permute-start(f32[200,768]{1,0:T(8,128)S(1)} %add.1200), channel_id=1, source_target_pairs={{0,1},{1,0},{2,3},{3,2},{4,5},{5,4},{6,7},{7,6},{8,9},{9,8},{10,11... | collective-permute-start | bytes 1843208 | tf_op jit(solution)/shard_map/ppermute | solution.py:67
  395.6 92.2 %collective-permute-start.23 = (f32[200,768]{1,0:T(8,128)}, f32[200,768]{1,0:T(8,128)}, u32[]{:S(2)}, u32[]{:S(2)}) collective-permute-start(f32[200,768]{1,0:T(8,128)} %add.1168), channel_id=1, source_target_pairs={{0,1},{1,0},{2,3},{3,2},{4,5},{5,4},{6,7},{7,6},{8,9},{9,8},{10,11... | collective-permute-start | bytes 1843208 | tf_op jit(solution)/shard_map/ppermute | solution.py:67
  463.8 26.5 %collective-permute-start.27 = (f32[200,768]{1,0:T(8,128)}, f32[200,768]{1,0:T(8,128)}, u32[]{:S(2)}, u32[]{:S(2)}) collective-permute-start(f32[200,768]{1,0:T(8,128)} %slice_select_fusion.6), channel_id=1, source_target_pairs={{0,1},{1,0},{2,3},{3,2},{4,5},{5,4},{6,7},{7,6},{8,9},{9,8},{10,11... | collective-permute-start | bytes 1843208 | tf_op jit(solution)/shard_map/ppermute | solution.py:65
  487.3 6.6 collective-permute-start.39
  492.4 17.0 %collective-permute-start.28 = (f32[200,768]{1,0:T(8,128)}, f32[200,768]{1,0:T(8,128)}, u32[]{:S(2)}, u32[]{:S(2)}) collective-permute-start(f32[200,768]{1,0:T(8,128)} %select_add_fusion.6), channel_id=1, source_target_pairs={{0,2},{2,0},{1,3},{3,1},{4,6},{6,4},{5,7},{7,5},{8,10},{10,8},{9,1... | collective-permute-start | bytes 1843208 | tf_op jit(solution)/shard_map/ppermute | solution.py:66
  496.0 26.0 %collective-permute-start.40 = (f32[200,768]{1,0:T(8,128)}, f32[200,768]{1,0:T(8,128)}, u32[]{:S(2)}, u32[]{:S(2)}) collective-permute-start(f32[200,768]{1,0:T(8,128)} %select_add_fusion.2), channel_id=1, source_target_pairs={{0,2},{2,0},{1,3},{3,1},{4,6},{6,4},{5,7},{7,5},{8,10},{10,8},{9,1... | collective-permute-start | bytes 1843208 | tf_op jit(solution)/shard_map/ppermute | solution.py:66
  497.0 13.8 %copy-start.49 = (f32[400,576]{0,1:T(8,128)S(1)}, f32[400,576]{0,1:T(8,128)}, u32[]{:S(2)}) copy-start(f32[400,576]{0,1:T(8,128)} %constant_dynamic-update-slice_fusion) | copy-start | bytes 2764804
  510.7 15.8 %collective-permute-start.29 = (f32[200,768]{1,0:T(8,128)S(1)}, f32[200,768]{1,0:T(8,128)S(1)}, u32[]{:S(2)}, u32[]{:S(2)}) collective-permute-start(f32[200,768]{1,0:T(8,128)S(1)} %add.1181), channel_id=1, source_target_pairs={{0,1},{1,0},{2,3},{3,2},{4,5},{5,4},{6,7},{7,6},{8,9},{9,8},{10,11... | collective-permute-start | bytes 1843208 | tf_op jit(solution)/shard_map/ppermute | solution.py:67
  523.3 3.4 collective-permute-start.41
  552.4 228.4 %reduce-scatter.19.cloned.1.call-start = ((), (), s32[]{:S(2)}) async-start(), calls=%async_computation.9 | async-start | bytes 5308416
  562.4 8.6 collective-permute-start.30
  567.1 5.6 collective-permute-start.42
  571.1 16.8 %collective-permute-start.31 = (f32[200,768]{1,0:T(8,128)S(1)}, f32[200,768]{1,0:T(8,128)S(1)}, u32[]{:S(2)}, u32[]{:S(2)}) collective-permute-start(f32[200,768]{1,0:T(8,128)S(1)} %select_add_fusion.5), channel_id=1, source_target_pairs={{0,2},{2,0},{1,3},{3,1},{4,6},{6,4},{5,7},{7,5},{8,10},{10,8},{9,1... | collective-permute-start | bytes 1843208 | tf_op jit(solution)/shard_map/ppermute | solution.py:66
  572.8 27.3 %collective-permute-start.43 = (f32[200,768]{1,0:T(8,128)S(1)}, f32[200,768]{1,0:T(8,128)S(1)}, u32[]{:S(2)}, u32[]{:S(2)}) collective-permute-start(f32[200,768]{1,0:T(8,128)S(1)} %select_add_fusion.1), channel_id=1, source_target_pairs={{0,2},{2,0},{1,3},{3,1},{4,6},{6,4},{5,7},{7,5},{8,10},{10,8},{9,1... | collective-permute-start | bytes 1843208 | tf_op jit(solution)/shard_map/ppermute | solution.py:66
  573.4 14.7 %copy-start.118 = (f32[400,768]{1,0:T(8,128)S(1)}, f32[400,768]{1,0:T(8,128)}, u32[]{:S(2)}) copy-start(f32[400,768]{1,0:T(8,128)} %copy-done.117) | copy-start | bytes 3686404
  588.0 21.3 %collective-permute-start.32 = (f32[200,768]{1,0:T(8,128)S(1)}, f32[200,768]{1,0:T(8,128)S(1)}, u32[]{:S(2)}, u32[]{:S(2)}) collective-permute-start(f32[200,768]{1,0:T(8,128)S(1)} %add.1188), channel_id=1, source_target_pairs={{0,1},{1,0},{2,3},{3,2},{4,5},{5,4},{6,7},{7,6},{8,9},{9,8},{10,11... | collective-permute-start | bytes 1843208 | tf_op jit(solution)/shard_map/ppermute | solution.py:67
  600.2 9.3 %collective-permute-start.44 = (f32[200,768]{1,0:T(8,128)S(1)}, f32[200,768]{1,0:T(8,128)S(1)}, u32[]{:S(2)}, u32[]{:S(2)}) collective-permute-start(f32[200,768]{1,0:T(8,128)S(1)} %add.1213), channel_id=1, source_target_pairs={{0,1},{1,0},{2,3},{3,2},{4,5},{5,4},{6,7},{7,6},{8,9},{9,8},{10,11... | collective-permute-start | bytes 1843208 | tf_op jit(solution)/shard_map/ppermute | solution.py:67
  609.1 205.8 %reduce-scatter.13.cloned.1.call-start = ((), (), s32[]{:S(2)}) async-start(), calls=%async_computation.6 | async-start | bytes 3096576
  651.2 46.9 %collective-permute-start.33 = (f32[200,768]{1,0:T(8,128)}, f32[200,768]{1,0:T(8,128)}, u32[]{:S(2)}, u32[]{:S(2)}) collective-permute-start(f32[200,768]{1,0:T(8,128)} %slice_select_fusion.4), channel_id=1, source_target_pairs={{0,1},{1,0},{2,3},{3,2},{4,5},{5,4},{6,7},{7,6},{8,9},{9,8},{10,11... | collective-permute-start | bytes 1843208 | tf_op jit(solution)/shard_map/ppermute | solution.py:65
  688.6 13.0 %collective-permute-start.45 = (f32[200,768]{1,0:T(8,128)}, f32[200,768]{1,0:T(8,128)}, u32[]{:S(2)}, u32[]{:S(2)}) collective-permute-start(f32[200,768]{1,0:T(8,128)} %slice_select_fusion), channel_id=1, source_target_pairs={{0,1},{1,0},{2,3},{3,2},{4,5},{5,4},{6,7},{7,6},{8,9},{9,8},{10,11... | collective-permute-start | bytes 1843208 | tf_op jit(solution)/shard_map/ppermute | solution.py:65
  700.1 17.0 %collective-permute-start.34 = (f32[200,768]{1,0:T(8,128)}, f32[200,768]{1,0:T(8,128)}, u32[]{:S(2)}, u32[]{:S(2)}) collective-permute-start(f32[200,768]{1,0:T(8,128)} %select_add_fusion.4), channel_id=1, source_target_pairs={{0,2},{2,0},{1,3},{3,1},{4,6},{6,4},{5,7},{7,5},{8,10},{10,8},{9,1... | collective-permute-start | bytes 1843208 | tf_op jit(solution)/shard_map/ppermute | solution.py:66
  703.7 25.7 %collective-permute-start.46 = (f32[200,768]{1,0:T(8,128)}, f32[200,768]{1,0:T(8,128)}, u32[]{:S(2)}, u32[]{:S(2)}) collective-permute-start(f32[200,768]{1,0:T(8,128)} %select_add_fusion), channel_id=1, source_target_pairs={{0,2},{2,0},{1,3},{3,1},{4,6},{6,4},{5,7},{7,5},{8,10},{10,8},{9,1... | collective-permute-start | bytes 1843208 | tf_op jit(solution)/shard_map/ppermute | solution.py:66
  718.5 15.4 %collective-permute-start.35 = (f32[200,768]{1,0:T(8,128)S(1)}, f32[200,768]{1,0:T(8,128)S(1)}, u32[]{:S(2)}, u32[]{:S(2)}) collective-permute-start(f32[200,768]{1,0:T(8,128)S(1)} %add.1194), channel_id=1, source_target_pairs={{0,1},{1,0},{2,3},{3,2},{4,5},{5,4},{6,7},{7,6},{8,9},{9,8},{10,11... | collective-permute-start | bytes 1843208 | tf_op jit(solution)/shard_map/ppermute | solution.py:67
  730.7 3.3 collective-permute-start.47
  745.1 167.9 %reduce-scatter.17.cloned.1.call-start = ((), (), s32[]{:S(2)}) async-start(), calls=%async_computation.8 | async-start | bytes 5308416
  781.9 35.2 %slice-start = ((f32[4,2,3,8]{3,2,1,0:T(4,128)}), f32[1,2,3,8]{3,2,1,0:T(4,128)S(1)}, s32[]{:S(2)}) async-start(f32[4,2,3,8]{3,2,1,0:T(4,128)} %copy-done.188), calls=%async_computation.10 | async-start | bytes 8192 | tf_op jit(solution)/shard_map/slice | solution.py:278
  (199 other events, 571.7 us)
Sparse Core Ops, SparseCore 0:
  17.0 70.3 all-gather.2
  168.6 66.2 all-gather.4
  552.6 69.3 reduce-scatter.14
  625.5 94.2 reduce-scatter.18
  745.2 69.6 reduce-scatter.12
  818.4 94.4 reduce-scatter.16
